TPU v7x, 128 devices: a whole 4x4x4 slice. The times are simulated.
128 devices in a mesh: seq: 16 (over z, y), head: 8 (over x, core).
Axes of the slice: x: 4, y: 4, z: 4, core: 2. Of those that a mesh axis runs over, the one named last changes fastest.
Arguments:
- tokens: bfloat16 [8192, 2048], P(('seq', 'head')), may hold values from -6 to 6
- mixer_gain: float32 [2048], replicated, may hold values from 0.5 to 1.5
- mixer_weight: bfloat16 [2048, 16, 768], P(None, 'head'), may hold values from -0.125 to 0.125
- rate_weight: bfloat16 [2048, 2, 16], P(None, None, 'head'), may hold values from -0.125 to 0.125
- conv_weight: bfloat16 [4, 16, 512], P(None, 'head'), may hold values from -3 to 3
- decay_log: float32 [16], P('head')
- decay_bias: float32 [16], P('head'), may hold values from -2 to 1
- head_gain: float32 [256], replicated, may hold values from 0.5 to 1.5
- output_weight: bfloat16 [16, 256, 2048], P('head'), may hold values from -0.1875 to 0.1875
- feed_gain: float32 [2048], replicated, may hold values from 0.5 to 1.5
- gate_up_weight: bfloat16 [2048, 2, 5504], P(None, None, 'head'), may hold values from -0.125 to 0.125
- down_weight: bfloat16 [5504, 2048], P('head'), may hold values from -0.15625 to 0.15625
- doc_starts: int32 [4], replicated, may hold values from 1 to 8191, as said below
- cotangent: bfloat16 [8192, 2048], P(('seq', 'head')), may hold values from -6 to 6
Outputs:
- layer_out: bfloat16 [8192, 2048], P(('seq', 'head'))
- grad_tokens: float32 [8192, 2048], P(('seq', 'head'))
- grad_mixer_gain: float32 [2048], replicated
- grad_mixer_weight: float32 [2048, 16, 768], P('seq', 'head')
- grad_rate_weight: float32 [2048, 2, 16], P('seq', None, 'head')
- grad_conv_weight: float32 [4, 16, 512], P(None, 'head')
- grad_decay_log: float32 [16], P('head')
- grad_decay_bias: float32 [16], P('head')
- grad_head_gain: float32 [256], replicated
- grad_output_weight: float32 [16, 256, 2048], P('head', None, 'seq')
- grad_feed_gain: float32 [2048], replicated
- grad_gate_up_weight: float32 [2048, 2, 5504], P('seq', None, 'head')
- grad_down_weight: float32 [5504, 2048], P('head', 'seq')
Inputs may be any that keep to these rules, and one draw needn't show every extreme that they name: `doc_starts`: 4 increasing positions at which a new document begins: the first two lie within the first 512 positions, the last two within the last 512 positions.
All inputs are finite; a program needn't handle non-finite values.
Results may differ from a plain program's by a relative error of at most 0.022.
The roundings to bfloat16 on the way count: a program that leaves them out, or rounds other values in their place, can miss the bound.
Values may be sent and summed in bfloat16 or wider, within the bound.
A program may use at most 192 MiB of HBM per device.

v0:
```python
import functools

import jax
import jax.numpy as jnp
from jax import lax
from jax.experimental import pallas as pl
from jax.experimental.pallas import tpu as pltpu
from jax.sharding import PartitionSpec as P

D = 2048
DK = 128
DV = 256
KCONV = 4
MIXW = 768
CONVW = 512
NB = 4
BLK = 256
PAD = 8
F32 = jnp.float32
BF16 = jnp.bfloat16

VMEM = pl.BlockSpec(memory_space=pltpu.VMEM)
SMEM = pl.BlockSpec(memory_space=pltpu.SMEM)


def dot(a, b, form="nn"):
    dims = {"nn": ((1,), (0,)), "nt": ((1,), (1,)), "tn": ((0,), (0,))}[form]
    return lax.dot_general(a.astype(BF16), b.astype(BF16), (dims, ((), ())), preferred_element_type=F32)


def halves(a):
    hi = a.astype(BF16)
    return hi, (a - hi.astype(F32)).astype(BF16)


def dot3(a, b, form="nn"):
    ah, al = halves(a)
    bh, bl = halves(b)
    return dot(ah, bh, form) + (dot(ah, bl, form) + dot(al, bh, form))


def dot_exact_left(a, b, form="nn"):
    b1, rest = halves(b)
    rest = b - b1.astype(F32)
    b2 = rest.astype(BF16)
    b3 = (rest - b2.astype(F32)).astype(BF16)
    return dot(a, b1, form) + (dot(a, b2, form) + dot(a, b3, form))


def iota(shape, axis):
    return lax.broadcasted_iota(jnp.int32, shape, axis)


def doc_of(info, pos):
    count = jnp.zeros(pos.shape, jnp.int32)
    for i in range(NB):
        count = count + jnp.where(pos >= info[i], 1, 0)
    return jnp.where(pos < 0, -1, count)


def sigmoid(v):
    return 1.0 / (1.0 + jnp.exp(-v))


def softplus(v):
    return jnp.maximum(v, 0.0) + jnp.log1p(jnp.exp(-jnp.abs(v)))


def unit_lower_inverse(low):
    n = low.shape[0]
    row, col = iota((n, n), 0), iota((n, n), 1)
    eye = jnp.where(row == col, 1.0, 0.0)

    def same(b):
        return row // b == col // b

    x = jnp.where(same(8), -low, 0.0)
    inv = eye + x
    x = dot(x, x)
    inv = inv + dot(inv, x)
    x = dot(x, x)
    inv = inv + dot(inv, x)
    b = 8
    while b < n:
        off = jnp.where(same(2 * b) & jnp.logical_not(same(b)), low, 0.0)
        inv = inv - dot(inv, dot(off, inv))
        b *= 2
    return inv + dot(inv, eye - inv - dot3(low, inv))


def valid_column(info, rows, back):
    pos = info[NB] + iota((rows, 1), 0)
    return jnp.where(doc_of(info, pos) == doc_of(info, pos - back), 1.0, 0.0)


def vectors(conv):
    act = conv * sigmoid(conv)
    qa, ka, va = act[:, :DK], act[:, DK : 2 * DK], act[:, 2 * DK :]
    rq = lax.rsqrt(jnp.sum(qa * qa, axis=1, keepdims=True) + 1e-06)
    rk = lax.rsqrt(jnp.sum(ka * ka, axis=1, keepdims=True) + 1e-06)
    return qa, ka, va, rq, rk


def rates(rate_ref, dlog_ref, dbias_ref):
    heads = dlog_ref.shape[1]
    pre = rate_ref[:, :heads] + dbias_ref[...]
    log_decay = -jnp.exp(dlog_ref[...]) * softplus(pre)
    return sigmoid(rate_ref[:, heads:]), log_decay, pre


def block_masks(info, c):
    row, col = iota((BLK, BLK), 0), iota((BLK, BLK), 1)
    base = info[NB] + c * BLK
    docs_r, docs_c = doc_of(info, base + row), doc_of(info, base + col)
    keep = (docs_r == docs_c) & (col <= row)
    column = doc_of(info, base + iota((BLK, 1), 0))
    first = jnp.where(column == doc_of(info, base - 1 + iota((BLK, 1), 0) * 0), 1.0, 0.0)
    last = jnp.where(column == doc_of(info, base + BLK - 1 + iota((BLK, 1), 0) * 0), 1.0, 0.0)
    tri = jnp.where(col <= row, 1.0, 0.0)
    strict = jnp.where(col < row, 1.0, 0.0)
    return keep, first, last, tri, strict


def decays(g, first, last, tri):
    cum = dot_exact_left(tri, jnp.broadcast_to(g, (BLK, DK)))[:, :1]
    carry = first * jnp.exp(cum)
    to_end = last * jnp.exp(cum[BLK - 1 :, :] - cum)
    return carry, to_end


def mixer_forward(
    info, proj, rate, convw, dlog, dbias, out_w, gain, cot,
    conv_o, dec_o, inv_o, wu_o, qe_o, step_o, states_o, head_o, gated_o, ga_o, ta_o, halo_o, mixed_o, cot_o,
    xpad, ol, gs, scores, ab, rim, rim_got, got1, tot, got2, hs, hr, s1, r1, s2, r2, sc, rc, lc
):
    rows = proj.shape[0]
    heads = dlog.shape[1]
    blocks = rows // BLK
    me, z, y, dev = seq_place()
    seqs, head = SIDE * SIDE, lax.axis_index("head")
    before, behind = (lax.rem(me + seqs - 1, seqs), head), (lax.rem(me + 1, seqs), head)
    greet(side_peers() + [before, behind] + head_peers())
    cot_sent = gather_start(cot, cot_o, sc, rc, lc)
    for h in range(heads):
        rim[:, pl.ds(h * CONVW, CONVW)] = proj[rows - PAD :, pl.ds(h * MIXW, CONVW)].astype(BF16).astype(F32)
    ahead = cp(rim, rim_got, hs, hr, behind)
    ahead.start()
    strength, log_decay, _ = rates(rate, dlog, dbias)
    valid = [valid_column(info, rows, KCONV - 1 - j) for j in range(KCONV)]
    ahead.wait_recv()
    halo_o[...] = jnp.where(me > 0, rim_got[...], 0.0)
    for h in range(heads):
        src, dst = pl.ds(h * MIXW, CONVW), pl.ds(h * CONVW, CONVW)
        xpad[:PAD, :] = halo_o[:, dst]
        xpad[PAD:, :] = proj[:, src].astype(BF16).astype(F32)
        conv = jnp.zeros((rows, CONVW), F32)
        for j in range(KCONV):
            lo = PAD - (KCONV - 1) + j
            conv = conv + convw[j : j + 1, dst].astype(F32) * xpad[lo : lo + rows, :] * valid[j]
        conv_o[:, dst] = conv
    for c in range(blocks):
        keep, first, last, tri, strict = block_masks(info, c)
        here = pl.ds(c * BLK, BLK)
        for h in range(heads):
            qa, ka, va, rq, rk = vectors(conv_o[here, pl.ds(h * CONVW, CONVW)])
            q, k = qa * (rq * DK**-0.5), ka * rk
            beta = strength[c * BLK : (c + 1) * BLK, h : h + 1]
            g = log_decay[c * BLK : (c + 1) * BLK, h : h + 1]
            spread = dot_exact_left(tri, g * strict)
            dec = jnp.where(keep, jnp.exp(jnp.where(keep, spread, 0.0)), 0.0)
            carry, to_end = decays(g, first, last, tri)
            low = strict * (beta * dec * dot(k, k, "nt"))
            inv = unit_lower_inverse(low)
            u = h * blocks + c
            dec_o[u] = dec
            inv_o[u] = inv.astype(BF16)
            rhs = jnp.concatenate([(beta * carry) * k, beta * va], axis=1)
            wu = dot(inv, rhs)
            wu_o[u] = wu
            scores[u] = (dec * dot(q, k, "nt")).astype(BF16)
            qe_o[here, pl.ds(h * DK, DK)] = carry * q
            step = dot(wu, to_end * k, "tn")
            eye = jnp.where(iota((DK, DK), 0) == iota((DK, DK), 1), 1.0, 0.0)
            step_o[u, :DK] = carry[BLK - 1 :, :] * eye - step[:DK]
            step_o[u, DK:] = step[DK:]
        if c == 0:
            cot_sent += gather_forward(cot, cot_o, sc, rc)
    for h in range(heads):
        whole = step_o[h * blocks]
        for c in range(1, blocks):
            nxt = step_o[h * blocks + c]
            whole = add_low(dot3(whole, nxt[:DK]), nxt[DK:])
        ab[h] = whole.astype(ab.dtype)

    out, wait = share_start(ab, got1, y, lambda d: dev(0, d), s1, r1)
    for h in range(heads):
        for c in range(blocks):
            u, here = h * blocks + c, pl.ds(c * BLK, BLK)
            block = dot(scores[u], wu_o[u])
            qe_o[here, pl.ds(h * DK, DK)] = qe_o[here, pl.ds(h * DK, DK)] - block[:, :DK]
            ol[here, pl.ds(h * DV, DV)] = block[:, DK:]
    wait()
    held_before = []
    for h in range(heads):
        whole = got1[0, h].astype(F32)
        prefix = jnp.where(y > 0, whole, unit_top())
        for j in range(1, SIDE):
            a, b = got1[j, h, :DK, :], got1[j, h, DK:, :].astype(F32)
            whole = add_low(dot_left2(whole, a), b)
            if j < SIDE - 1:
                prefix = jnp.where(y > j, whole, prefix)
        tot[h] = whole.astype(BF16)
        held_before.append(prefix)
        for j in range(SIDE):
            ga_o[j, h] = got1[j, h, :DK, :]
    more, wait = share_start(tot, got2, z, lambda d: dev(d, 0), s2, r2)
    for h in range(heads):
        gate = proj[:, pl.ds(h * MIXW + CONVW, DV)]
        gs[:, pl.ds(h * DV, DV)] = gain[...] * (gate * sigmoid(gate))
    wait()
    for h in range(heads):
        held = jnp.zeros((DV, DK), F32)
        for j in range(SIDE - 1):
            held = jnp.where(
                z > j, dot_left2(held, got2[j, h, :DK, :]) + got2[j, h, DK:, :].astype(F32), held
            )
        for j in range(SIDE):
            ta_o[j, h] = got2[j, h, :DK, :]
        state = dot3(held, held_before[h][:DK]) + held_before[h][DK:]
        for c in range(blocks):
            u = h * blocks + c
            here, cols = pl.ds(c * BLK, BLK), pl.ds(h * DV, DV)
            states_o[u] = state
            block = ol[here, cols] + dot(qe_o[here, pl.ds(h * DK, DK)], state, "nt")
            head_o[here, cols] = block
            gated_o[here, cols] = (block * mean_scale(block) * gs[here, cols]).astype(BF16)
            if c + 1 < blocks:
                state = dot3(state, step_o[u, :DK, :]) + step_o[u, DK:, :]
    for j in range(0, D, CONVW):
        mixed_o[:, j : j + CONVW] = dot(gated_o[...], out_w[:, j : j + CONVW]).astype(BF16)
    gather_end(cot, cot_o, sc, rc, lc, cot_sent)
    for s in out + more + [ahead]:
        s.wait_send()


def dot_left2(a, b, form="nn"):
    ah, al = halves(a)
    return dot(ah, b, form) + dot(al, b, form)


def head_back(d_mixed, out_w, head_out, proj, gain, qe, step, d_out_o, d_gate_o, y_o, inc_o):
    rows = qe.shape[0]
    blocks = rows // BLK
    heads = qe.shape[1] // DK
    total = jnp.zeros((1, DV), F32)
    for h in range(heads):
        cols = pl.ds(h * DV, DV)
        for c in range(blocks):
            here = pl.ds(c * BLK, BLK)
            dg, out = dot(d_mixed[here, :], out_w[cols, :], "nt"), head_out[here, cols]
            gate = proj[here, pl.ds(h * MIXW + CONVW, DV)]
            s = sigmoid(gate)
            silu = gate * s
            scale = lax.rsqrt(jnp.mean(out * out, axis=1, keepdims=True) + 1e-05)
            dn = dg * (out * scale)
            d_gate_o[here, pl.ds(h * MIXW + CONVW, DV)] = (dn * gain[...] * (s * (1.0 + gate * (1.0 - s)))).astype(BF16)
            total = total + jnp.sum(dn * silu, axis=0, keepdims=True)
            f = dg * gain[...] * silu
            d_out = scale * f - out * (scale * scale * scale) * jnp.mean(f * out, axis=1, keepdims=True)
            d_out_o[here, cols] = d_out
            y_o[h * blocks + c] = dot(d_out, qe[here, pl.ds(h * DK, DK)], "tn")
        inc = y_o[h * blocks + blocks - 1]
        for c in range(blocks - 2, -1, -1):
            inc = y_o[h * blocks + c] + dot3(inc, step[h * blocks + c, :DK, :], "nt")
        inc_o[h] = inc.astype(inc_o.dtype)
    return total


def mixer_back(
    info, d_mixed, out_w, head_out, proj, gain, qe, step, ga, ta, middle, cot, gated_t, s_gu, conv, dec, inv, wu, states,
    rate, halo, convw, dlog, dbias,
    d_proj_o, d_tail_o, d_edge_o, d_rate_o, d_convw_o, d_decay_o, d_gain_o, s_down_o, s_out_o, g_gu_o,
    d_out, y, inc, later, got1, tot, got2, xpad, dpad, dsend, cols_s, d_pre_o,
    g_down, g_out, relay_d, relay_o, got_d, got_o, last_got, s1, r1, s2, r2, s3, r3, s4, r4
):
    greet(side_peers())
    settle = Settle(lambda i, b: last_got.at[i, b], s4, r4)
    for b in (2, 1, 3):
        for i in range(2):
            settle.send(s_gu.at[i, b], i, b)
    grads = (g_down, g_out)
    spread = Spread(
        lambda i, owner: grads[i].at[owner], lambda i, b: (relay_d, relay_o)[i].at[b],
        lambda i, s, b: (got_d, got_o)[i].at[s, b], s3, r3,
    )
    d_gain_o[...] = head_back(d_mixed, out_w, head_out, proj, gain, qe, step, d_out, d_proj_o, y, inc)

    def make(o, left, right):
        for j in range(0, o.shape[0], 2):
            both = dot(left[...], right[:, j * LANES : (j + 2) * LANES]).astype(BF16)
            o[j], o[j + 1] = both[:, :LANES], both[:, LANES:]

    def level_one():
        make(g_down, middle, cot)
        make(g_out, gated_t, d_mixed)

    def level_two():
        for place in PLACES:
            spread.ready(*place, (0,))

    swaps = states_backward(inc, ga, ta, later, got1, tot, got2, s1, r1, s2, r2, level_one, level_two)
    for place in PLACES:
        spread.ready(*place, (1,))
    rows = d_out.shape[0]
    heads = later.shape[0]
    blocks = rows // BLK
    strength, log_decay, pre = rates(rate, dlog, dbias)
    valid = [valid_column(info, rows, KCONV - 1 - j) for j in range(KCONV)]
    for h in range(heads):
        grad = later[h]
        for c in range(blocks - 1, -1, -1):
            u = h * blocks + c
            dsend[u] = grad
            if c:
                grad = dot3(grad, step[u, :DK, :], "nt") + y[u]
    for c in range(blocks):
        keep, first, last, tri, strict = block_masks(info, c)
        here = pl.ds(c * BLK, BLK)
        for h in range(heads):
            u = h * blocks + c
            cv = conv[here, pl.ds(h * CONVW, CONVW)]
            sg = sigmoid(cv)
            qa, ka, va, rq, rk = vectors(cv)
            rqs = rq * DK**-0.5
            q, k = qa * rqs, ka * rk
            beta = strength[c * BLK : (c + 1) * BLK, h : h + 1]
            g = log_decay[c * BLK : (c + 1) * BLK, h : h + 1]
            carry, to_end = decays(g, first, last, tri)
            dm = dec[u]
            sc = dm * dot3(q, k, "nt")
            gm = dm * dot3(k, k, "nt") * strict
            state, d_end = states[u], dsend[u]
            do = d_out[here, pl.ds(h * DV, DV)]
            ks = dot3(k, state, "nt")
            qs = dot3(q, state, "nt")
            fresh = wu[u, :, DK:] - dot3(wu[u, :, :DK], state, "nt")
            kd = to_end * k
            d_fresh = dot(sc, do, "tn") + dot(kd, d_end, "nt")
            ah, al = halves(d_fresh)
            d_rhs = dot(inv[u], ah, "tn") + dot(inv[u], al, "tn")
            d_low = -dot3(d_rhs, fresh, "nt")
            d_sc = dot3(do, fresh, "nt")
            d_val = beta * d_rhs
            ebar = d_low * gm
            d_beta = jnp.sum(d_rhs * (va - carry * ks), axis=1, keepdims=True) + jnp.sum(ebar, axis=1, keepdims=True)
            e = d_sc * sc + beta * ebar
            d_scd = d_sc * dm
            d_gm = (beta * d_low) * (dm * strict)
            d_kd = dot(fresh, d_end)
            d_q = dot(d_scd, k) + carry * dot(do, state)
            d_k = (
                dot(d_scd, q, "tn")
                - (beta * carry) * dot(d_rhs, state)
                + to_end * d_kd
                + dot(d_gm, k)
                + dot(d_gm, k, "tn")
            )
            hcol = carry * jnp.sum(do * qs - beta * d_rhs * ks, axis=1, keepdims=True)
            fcol = jnp.sum(kd * d_kd, axis=1, keepdims=True)
            tail = carry[BLK - 1 :, :] * jnp.sum(
                jnp.sum(state * d_end, axis=1, keepdims=True), axis=0, keepdims=True
            )
            lane = iota((BLK, DK), 1)
            d_g = (
                jnp.sum(dot_exact_left(tri, e, "tn") * strict, axis=1, keepdims=True)
                + dot_exact_left(tri, jnp.where(lane == 0, hcol, 0.0), "tn")[:, :1]
                + dot_exact_left(strict, jnp.where(lane == 0, fcol, 0.0))[:, :1]
                + tail
            )
            cols_s[here, h : h + 1] = d_g
            cols_s[here, heads + h : heads + h + 1] = d_beta
            d_qa = rqs * d_q - qa * (rqs * rq * rq * jnp.sum(d_q * qa, axis=1, keepdims=True))
            d_ka = rk * d_k - ka * (rk * rk * rk * jnp.sum(d_k * ka, axis=1, keepdims=True))
            d_act = jnp.concatenate([d_qa, d_ka, d_val], axis=1)
            d_pre_o[here, pl.ds(h * CONVW, CONVW)] = d_act * (sg * (1.0 + cv * (1.0 - sg)))
            spread.relays(c * heads + h)
    d_g, d_beta = cols_s[:, :heads], cols_s[:, heads : 2 * heads]
    d_bias = -d_g * jnp.exp(dlog[...]) * sigmoid(pre)
    rest = jnp.zeros((rows, LANES - 2 * heads), F32)
    d_rate_o[...] = jnp.concatenate([d_bias, d_beta * strength * (1.0 - strength), rest], axis=1).astype(BF16)
    d_decay_o[...] = jnp.zeros_like(d_decay_o)
    d_decay_o[:, :heads] = jnp.sum(d_g * log_decay, axis=0, keepdims=True)
    d_decay_o[:, heads : 2 * heads] = jnp.sum(d_bias, axis=0, keepdims=True)
    for h in range(heads):
        src, dst = pl.ds(h * MIXW, CONVW), pl.ds(h * CONVW, CONVW)
        xpad[:PAD, :] = halo[:, dst]
        xpad[PAD:, :] = proj[:, src].astype(BF16).astype(F32)
        dpad[...] = jnp.zeros_like(dpad)
        d_conv = d_pre_o[:, dst]
        for j in range(KCONV):
            lo = PAD - (KCONV - 1) + j
            masked = d_conv * valid[j]
            d_convw_o[j : j + 1, dst] = jnp.sum(masked * xpad[lo : lo + rows, :], axis=0, keepdims=True)
            dpad[lo : lo + rows, :] += convw[j : j + 1, dst].astype(F32) * masked
        d_edge_o[:, dst] = dpad[:PAD, :]
        d_tail_o[:, dst] = dpad[rows - PAD :, :]
        d_proj_o[:, src] = dpad[PAD:, :].astype(BF16)
    for i in range(2):
        g_gu_o[i] = s_gu[i, 0].astype(F32) + settle.others(i)
    for i, o in ((0, s_down_o), (1, s_out_o)):
        for b in FAR:
            o[b] = spread.total(i, b).astype(BF16)
    spread.end()
    settle.end()
    for s in swaps:
        s.wait_send()


def call(kernel, outs, scratch, limit, *args, flops=2_000_000_000, nbytes=16_000_000):
    def spec(a):
        return SMEM if a.dtype == jnp.int32 else VMEM

    return pl.pallas_call(
        kernel,
        out_shape=outs,
        in_specs=[spec(a) for a in args],
        out_specs=[VMEM for _ in outs],
        scratch_shapes=scratch,
        compiler_params=pltpu.CompilerParams(vmem_limit_bytes=limit << 20),
        cost_estimate=pl.CostEstimate(flops=flops, bytes_accessed=nbytes, transcendentals=0),
    )(*args)


def sds(shape, dtype=F32):
    return jax.ShapeDtypeStruct(shape, dtype)
CHIPS = 4
LANES = 128


def cp(src, dst, send, recv, dev):
    return pltpu.make_async_remote_copy(
        src_ref=src, dst_ref=dst, send_sem=send, recv_sem=recv, device_id=dev, device_id_type=pl.DeviceIdType.MESH
    )


def greet(devices):
    barrier = pltpu.get_barrier_semaphore()
    for dev in devices:
        pl.semaphore_signal(barrier, inc=1, device_id=dev, device_id_type=pl.DeviceIdType.MESH)
    pl.semaphore_wait(barrier, len(devices))


def head_place():
    me = lax.axis_index("head")
    chip, core = me // 2, me % 2
    seq = lax.axis_index("seq")

    def dev(step, flip=False):
        c = lax.rem(chip + step, CHIPS)
        return (seq, c * 2 + (1 - core if flip else core))

    return me, chip, core, dev


def head_peers():
    dev = head_place()[3]
    return [dev(0, True)] + [dev(d) for d in range(1, CHIPS)]


def head_rows(o, rows, step, flip=False, lo=0, size=None):
    owner = head_place()[3](step, flip)[1]
    size = size or rows
    return o.at[pl.ds(pl.multiple_of(owner * rows + lo, size), size)]


def gather_start(x, o, ssem, rsem, lsem):
    rows = x.shape[0]
    dev = head_place()[3]
    pltpu.make_async_copy(x, head_rows(o, rows, 0), lsem).start()
    out = [cp(x, head_rows(o, rows, 0), ssem.at[d], rsem.at[d], dev(d)) for d in (1, 3)]
    out.append(cp(x, head_rows(o, rows, 0), ssem.at[0], rsem.at[0], dev(0, True)))
    for s in out:
        s.start()
    return out


def opposite(rows):
    return ((0, 2, 6, 1), (rows // 2, 8, 9, 3))


def gather_forward(x, o, ssem, rsem):
    rows = x.shape[0]
    dev = head_place()[3]
    partner = dev(0, True)
    out = []

    def go(src, k, to):
        s = cp(src, src, ssem.at[k], rsem.at[k], to)
        s.start()
        out.append(s)

    for lo, relay, core, step in opposite(rows):
        there = head_rows(o, rows, CHIPS - step)
        cp(x, there, ssem.at[step], rsem.at[step], dev(step)).wait_recv()
        go(head_rows(o, rows, CHIPS - step, False, lo, rows // 2), relay, dev(step))
        go(there, CHIPS + step, partner)
    for lo, relay, core, step in opposite(rows):
        there = head_rows(o, rows, 2, False, lo, rows // 2)
        cp(there, there, ssem.at[relay], rsem.at[relay], dev(step)).wait_recv()
        go(there, core, partner)
    return out


def gather_end(x, o, ssem, rsem, lsem, sent):
    rows = x.shape[0]
    dev = head_place()[3]
    partner = dev(0, True)
    pltpu.make_async_copy(x, head_rows(o, rows, 0), lsem).wait()
    cp(x, head_rows(o, rows, 0, True), ssem.at[0], rsem.at[0], partner).wait_recv()
    for lo, relay, core, step in opposite(rows):
        k = CHIPS + step
        cp(x, head_rows(o, rows, CHIPS - step, True), ssem.at[k], rsem.at[k], partner).wait_recv()
        there = head_rows(o, rows, 2, True, lo, rows // 2)
        cp(there, there, ssem.at[core], rsem.at[core], partner).wait_recv()
    for s in sent:
        s.wait_send()


def mean_scale(v):
    return lax.rsqrt(jnp.mean(v * v, axis=1, keepdims=True) + 1e-05)


def first_norm(tokens, gain, all_o, block, ssem, rsem, lsem):
    greet(head_peers())
    v = tokens[...].astype(F32)
    block[...] = (v * mean_scale(v) * gain[...]).astype(BF16)
    sent = gather_start(block, all_o, ssem, rsem, lsem)
    sent += gather_forward(block, all_o, ssem, rsem)
    gather_end(block, all_o, ssem, rsem, lsem, sent)


def norm_back(v, gain, d_norm):
    r = mean_scale(v)
    e = d_norm * gain
    d_v = r * e - v * (r * r * r * jnp.mean(e * v, axis=1, keepdims=True))
    return d_v, jnp.sum(d_norm * v * r, axis=0, keepdims=True)


def feed_forward(
    x, tokens, gain, cot, cot_all, gu, down,
    hidden_o, all_o, d_hidden_o, d_gain_o, sums_o, middle_o, feed_o,
    n2, guv, downv, d_middle, d_gu, d_two, block, ta, pa, ga, ma, tb, pb, gb, mb, g, relay, seqs_got,
    ls, sa, ra, sb, rb, s1, r1, l1, s2, r2, l2, s3, r3
):
    load_d = pltpu.make_async_copy(down, downv, ls.at[0])
    load_d.start()
    load_g = pltpu.make_async_copy(gu, guv, ls.at[1])
    load_g.start()
    greet(head_peers() + side_peers())
    one = pair_sends(x, pa, sa, ra, FAR)
    two = ChipSum(x, one, ta, pa, ga, ma, sa, ra)
    load_d.wait()
    d_middle[...] = dot(downv[...], cot_all[...], "nt")
    two.relay()
    hidden = tokens[...].astype(F32) + two.result()
    hidden_o[...] = hidden
    block[...] = (hidden * mean_scale(hidden) * gain[...]).astype(BF16)
    ahead = gather_start(block, n2, s1, r1, l1)
    load_g.wait()
    ahead += gather_forward(block, n2, s1, r1)
    gather_end(block, n2, s1, r1, l1, ahead)
    hid = downv.shape[0]
    low = hid // 32 * 16
    for lo, hi in ((0, low), (low, hid)):
        gate = dot(guv[lo:hi, :], n2[...], "nt")
        up = dot(guv[hid + lo : hid + hi, :], n2[...], "nt")
        s = sigmoid(gate)
        silu = gate * s
        dm = d_middle[lo:hi, :]
        middle_o[lo:hi, :] = (silu * up).astype(BF16)
        d_gu[lo:hi, :] = (dm * up * (s * (1.0 + gate * (1.0 - s)))).astype(BF16)
        d_gu[hid + lo : hid + hi, :] = (dm * silu).astype(BF16)
    for j in range(0, D, 512):
        d_two[:, j : j + 512] = dot(d_gu[...], guv[:, j : j + 512], "tn").astype(BF16)
    one_b = pair_sends(d_two, pb, sb, rb, FAR)
    spread = Spread(
        lambda i, owner: g.at[owner, i], lambda i, b: relay.at[i, b], lambda i, s, b: seqs_got.at[i, s, b], s3, r3
    )
    dev = seq_place()[3]

    def make(place):
        owner = dev(*place)[0]
        cols = n2[:, pl.ds(pl.multiple_of(owner * LANES, LANES), LANES)]
        out = dot(d_gu[...], cols).astype(BF16)
        g[owner, 0] = out[:hid]
        g[owner, 1] = out[hid:]
        spread.ready(*place)

    for place in PLACES[:3]:
        make(place)
    two_b = ChipSum(d_two, one_b, tb, pb, gb, mb, sb, rb)
    for place in PLACES[3:9]:
        make(place)
    two_b.relay()
    for place in PLACES[9:]:
        make(place)
    d_norm, d_gain = norm_back(hidden_o[...], gain[...], two_b.result())
    d_hidden = cot[...].astype(F32) + d_norm
    d_hidden_o[...] = d_hidden
    d_gain_o[...] = d_gain
    block[...] = d_hidden.astype(BF16)
    ahead = gather_start(block, all_o, s2, r2, l2)
    spread.relays()
    for j in range(0, D, 512):
        feed_o[:, j : j + 512] = dot(middle_o[...], downv[:, j : j + 512], "tn").astype(BF16)
    ahead += gather_forward(block, all_o, s2, r2)
    for b in FAR:
        for i in range(2):
            sums_o[i, b] = spread.total(i, b).astype(BF16)
    gather_end(block, all_o, s2, r2, l2, ahead)
    spread.end()
    two.end()
    two_b.end()


def reach(kernel, outs, scratch, cid, limit, *args, anywhere=(), scalars=(), nbytes=12_000_000):
    return pl.pallas_call(
        kernel,
        out_shape=outs,
        in_specs=[
            pl.BlockSpec(memory_space=pl.ANY) if i in anywhere else SMEM if i in scalars else VMEM for i in range(len(args))
        ],
        out_specs=[VMEM for _ in outs],
        scratch_shapes=scratch,
        compiler_params=pltpu.CompilerParams(
            collective_id=cid, has_side_effects=True, vmem_limit_bytes=limit << 20
        ),
        cost_estimate=pl.CostEstimate(flops=0, bytes_accessed=nbytes, transcendentals=0),
    )(*args)


def sems(n):
    return pltpu.SemaphoreType.DMA((n,))


def gather_scratch():
    return [sems(10), sems(10), pltpu.SemaphoreType.DMA]


SIDE = 4


def seq_place():
    me = lax.axis_index("seq")
    z, y = me // SIDE, me % SIDE
    head = lax.axis_index("head")

    def dev(dz, dy):
        return (lax.rem(z + dz, SIDE) * SIDE + lax.rem(y + dy, SIDE), head)

    return me, z, y, dev


def side_peers():
    dev = seq_place()[3]
    return [dev(0, d) for d in range(1, SIDE)] + [dev(d, 0) for d in range(1, SIDE)]


FAR = (2, 1, 3, 0)
FIRST, OTHER = (2, 1), (3, 0)
PLACES = (
    (2, 2), (2, 1), (1, 2), (2, 3), (3, 2), (2, 0), (0, 2), (1, 3), (3, 1), (1, 0), (0, 1), (3, 3), (1, 1), (0, 3), (3, 0),
    (0, 0),
)


class Spread:
    def __init__(self, piece, relay, got, ssem, rsem):
        self.piece, self.relay, self.got, self.ssem, self.rsem = piece, relay, got, ssem, rsem
        self.dev = seq_place()[3]
        self.sent = []

    def way(self, i, a, b):
        return self.dev(b, a) if i == 0 else self.dev(a, b)

    def copy(self, i, a, b, owner):
        k = (i * SIDE + a) * SIDE + b
        if a == 2:
            dst, step = self.relay(i, b), 1 if b in FIRST else 3
        else:
            dst, step = self.got(i, 0 if a == 1 else 1, b), a
        return cp(self.piece(i, owner), dst, self.ssem.at[k], self.rsem.at[k], self.way(i, step, 0))

    def send(self, i, a, b, owner):
        s = self.copy(i, a, b, owner)
        s.start()
        self.sent.append(s)

    def late(self, a, b):
        return a == 1 and b in FIRST or a == 3 and b in OTHER

    def ready(self, dz, dy, halves_=(0, 1)):
        owner = self.dev(dz, dy)[0]
        for i in halves_:
            a, b = (dy, dz) if i == 0 else (dz, dy)
            if a and not self.late(a, b):
                self.send(i, a, b, owner)

    def relays(self, part=None):
        for n, b in enumerate(FAR):
            if part is not None and n != part:
                continue
            for i in range(2):
                a = 1 if b in FIRST else 3
                owner = self.way(i, a, b)[0]
                self.copy(i, 2, b, owner).wait_recv()
                both = self.piece(i, owner)[...].astype(F32) + self.relay(i, b)[...].astype(F32)
                self.relay(i, b)[...] = both.astype(BF16)
                k = (i * SIDE + a) * SIDE + b
                s = cp(
                    self.relay(i, b), self.got(i, 0 if a == 1 else 1, b), self.ssem.at[k], self.rsem.at[k],
                    self.way(i, a, 0),
                )
                s.start()
                self.sent.append(s)

    def total(self, i, b):
        owner = self.way(i, 0, b)[0]
        for a in (1, 3):
            self.copy(i, a, b, owner).wait_recv()
        return self.piece(i, owner)[...].astype(F32) + (
            self.got(i, 0, b)[...].astype(F32) + self.got(i, 1, b)[...].astype(F32)
        )

    def end(self):
        for s in self.sent:
            s.wait_send()


class Settle:
    def __init__(self, got, ssem, rsem):
        self.got, self.ssem, self.rsem = got, ssem, rsem
        self.dev = seq_place()[3]
        self.sent = {}

    def send(self, src, i, b):
        k = i * SIDE + b
        dev = self.dev(b, 0) if i == 0 else self.dev(0, b)
        self.sent[i, b] = cp(src, self.got(i, b), self.ssem.at[k], self.rsem.at[k], dev)
        self.sent[i, b].start()

    def others(self, i):
        for b in (1, 3, 2):
            self.sent[i, b].wait_recv()
        return (self.got(i, 1)[...].astype(F32) + self.got(i, 3)[...].astype(F32)) + self.got(i, 2)[...].astype(F32)

    def end(self):
        for s in self.sent.values():
            s.wait_send()


def share_start(src, got, place, to, ssem, rsem, size=SIDE, own=None):
    part = (lambda d: src) if own is None else (lambda d: src.at[lax.rem(place + d, size)])
    got[place] = src[...] if own is None else src[place]
    steps = (2, 1, 3) if size == SIDE else range(1, size)
    out = [cp(part(d), got.at[place], ssem.at[d], rsem.at[d], to(d)) for d in steps]
    for s in out:
        s.start()

    def wait():
        for d in steps:
            back = lax.rem(place + size - d, size)
            cp(part(d), got.at[back], ssem.at[d], rsem.at[d], to(d)).wait_recv()

    return out, wait


def in_order(got):
    total = got[0]
    for i in range(1, got.shape[0]):
        total = total + got[i]
    return total


def share(src, got, place, to, ssem, rsem):
    out, wait = share_start(src, got, place, to, ssem, rsem)
    wait()
    return out


def unit_top():
    return jnp.where(iota((DK + DV, DK), 0) == iota((DK + DV, DK), 1), 1.0, 0.0)


def add_low(pair, low):
    return jnp.concatenate([pair[:DK], pair[DK:] + low], axis=0)


def states_backward(inc, ga, ta, later_o, got1, tot, got2, s1, r1, s2, r2, level_one, level_two):
    me, z, y, dev = seq_place()
    heads = inc.shape[0]
    out, wait = share_start(inc, got1, y, lambda d: dev(0, d), s1, r1)
    level_one()
    wait()
    after = []
    for h in range(heads):
        whole = add_low(dot(unit_top(), ga[SIDE - 1, h], "nt"), got1[SIDE - 1, h].astype(F32))
        suffix = jnp.where(y < SIDE - 1, whole, unit_top())
        for j in range(SIDE - 2, -1, -1):
            whole = add_low(dot_left2(whole, ga[j, h], "nt"), got1[j, h].astype(F32))
            if j:
                suffix = jnp.where(y < j, whole, suffix)
        tot[h] = whole[DK:].astype(BF16)
        after.append(suffix)
    more, wait = share_start(tot, got2, z, lambda d: dev(d, 0), s2, r2)
    level_two()
    wait()
    for h in range(heads):
        held = jnp.zeros((DV, DK), F32)
        for j in range(SIDE - 1, 0, -1):
            held = jnp.where(z < j, dot_left2(held, ta[j, h], "nt") + got2[j, h].astype(F32), held)
        later_o[h] = dot3(held, after[h][:DK]) + after[h][DK:]
    return out + more


def pair_sends(x, pair, ssem, rsem, steps):
    rows = pair.shape[1]
    dev = head_place()[3]
    out = {}
    for d in steps:
        owner = dev(d, True)[1]
        src = x.at[pl.ds(pl.multiple_of(owner * rows, rows), rows)]
        out[d] = cp(src, pair.at[d], ssem.at[d], rsem.at[d], dev(0, True))
        out[d].start()
    return out


class ChipSum:
    def __init__(self, x, first, total, pair, got, mid, ssem, rsem):
        self.x, self.first, self.total, self.pair = x, first, total, pair
        self.got, self.mid, self.ssem, self.rsem = got, mid, ssem, rsem
        self.rows = pair.shape[1]
        self.dev = head_place()[3]
        half = self.rows // 2
        self.top, self.low = slice(0, half), slice(half, self.rows)
        self.sent = []
        self.mid[2] = self.both(2).astype(BF16)
        self.send(2, self.top, 0, 4, 1)
        self.send(2, self.low, 0, 5, 3)
        self.right = self.both(1)
        self.mid[1, self.low] = self.right[self.low].astype(BF16)
        self.send(1, self.low, 1, 6, 1)
        self.left = self.both(3)
        self.mid[3, self.top] = self.left[self.top].astype(BF16)
        self.send(3, self.top, 3, 7, 3)
        self.total[...] = self.both(0)

    def both(self, d):
        self.first[d].wait_recv()
        owner = self.dev(d)[1]
        mine = self.x[pl.ds(pl.multiple_of(owner * self.rows, self.rows), self.rows), :]
        return mine.astype(F32) + self.pair[d].astype(F32)

    def copy(self, d, part, slot, k, step):
        at = pl.ds(part.start, part.stop - part.start)
        return cp(self.mid.at[d, at], self.got.at[slot, at], self.ssem.at[k], self.rsem.at[k], self.dev(step))

    def send(self, *what):
        s = self.copy(*what)
        s.start()
        self.sent.append(s)

    def relay(self):
        self.copy(2, self.top, 0, 4, 1).wait_recv()
        self.mid[1, self.top] = (self.right[self.top] + self.got[0, self.top].astype(F32)).astype(BF16)
        self.send(1, self.top, 1, 8, 1)
        self.copy(2, self.low, 0, 5, 3).wait_recv()
        self.mid[3, self.low] = (self.left[self.low] + self.got[0, self.low].astype(F32)).astype(BF16)
        self.send(3, self.low, 3, 9, 3)

    def result(self):
        self.copy(1, self.low, 1, 6, 1).wait_recv()
        self.copy(3, self.top, 3, 7, 3).wait_recv()
        self.copy(1, self.top, 1, 8, 1).wait_recv()
        self.copy(3, self.low, 3, 9, 3).wait_recv()
        return self.total[...] + (self.got[1].astype(F32) + self.got[3].astype(F32))

    def end(self):
        for s in self.sent + list(self.first.values()):
            s.wait_send()


def finish(
    dproj, normed, w, d_rate, rate_w, d_tail, d_edge, feed, hidden, tokens, d_hidden, gain, convs, decay, g_feed, g_head,
    s_down, s_out,
    layer_o, d_tokens_o, g_mixer_o, g_gain_o, g_feed_o, g_head_o, conv_o, dlog_o, dbias_o, rate_o, g_down_o, g_out_o,
    dp, wv, edge, g, relay, got1, mid, got2, dn, ta, pa, ga, ma, tb, pb, gb, mb, got_d, got_o,
    e0, eh, e1, ey, e2, ez, m0, mh, m1, my, m2, mz,
    es, er, ls, s1, r1, s2, r2, sa, ra, sb, rb, s5, r5, se, re, sm, rm
):
    me, z, y, dev = seq_place()
    head = lax.axis_index("head")
    heads, seqs = eh.shape[0], g.shape[1]
    rows = dp.shape[0]
    part, half = g_mixer_o.shape[1], g_mixer_o.shape[2]
    load_p = pltpu.make_async_copy(dproj, dp, ls.at[0])
    load_p.start()
    load_w = pltpu.make_async_copy(w, wv, ls.at[1])
    load_w.start()

    def across(d):
        return (me, lax.rem(head + d, heads))

    before, behind = (lax.rem(me + seqs - 1, seqs), head), (lax.rem(me + 1, seqs), head)
    greet([across(d) for d in range(1, heads)] + side_peers() + [before, behind])
    back = cp(d_edge, edge, es, er, before)
    back.start()
    feed_one = pair_sends(feed, pa, sa, ra, FAR)

    n_row, h_row = D // LANES, DV // LANES
    taps, wide_c = convs.shape
    c_row = wide_c // LANES
    ng, nc = e0.shape[0], taps * c_row + PAD
    for r in range(n_row):
        e0[r : r + 1, :] = g_feed[:, r * LANES : (r + 1) * LANES]
    e0[n_row:, :] = jnp.zeros((ng - n_row, LANES), F32)
    for r in range(h_row):
        e0[n_row + r : n_row + r + 1, :] = g_head[:, r * LANES : (r + 1) * LANES]
    small, wait_head = share_start(e0, eh, head, across, se.at[0], re.at[0], heads)
    for t in range(taps):
        for r in range(c_row):
            lo = ng + t * c_row + r
            e1[0, lo : lo + 1, :] = convs[t : t + 1, r * LANES : (r + 1) * LANES]
    e1[0, ng + nc - PAD : ng + nc, :] = jnp.zeros((PAD, LANES), F32)
    e1[0, ng + nc - PAD : ng + nc - PAD + 1, :] = decay[...]
    rates_t = dot(d_rate[:, :PAD], normed[...], "tn")
    for i in range(SIDE):
        if i:
            e1[i, ng : ng + nc, :] = e1[0, ng : ng + nc, :]
        for j in range(SIDE):
            at = (j * SIDE + i) * LANES
            e1[i, ng + nc + j * PAD : ng + nc + (j + 1) * PAD, :] = rates_t[:, at : at + LANES]

    sums = (s_down, s_out)
    settle = Settle(lambda i, b: (got_d, got_o)[i].at[b], s5, r5)
    for b in (2, 1, 3):
        for i in range(2):
            settle.send(sums[i].at[b], i, b)
    load_p.wait()
    back.wait_recv()
    there = jnp.where(me < seqs - 1, edge[...], 0.0)
    tail = jnp.concatenate([d_tail[:PAD, :], d_tail[PAD:, :] + there], axis=0).astype(BF16)
    wide = half - DV
    for i in range(2):
        dp[rows - 2 * PAD :, pl.ds(i * half, wide)] = tail[:, i * wide : (i + 1) * wide]

    spread = Spread(
        lambda i, owner: g.at[i, owner], lambda i, b: relay.at[i, b], lambda i, s, b: got1.at[i, s, b], s1, r1
    )
    settle_two = Settle(lambda i, b: got2.at[i, b], s2, r2)
    for n, place in enumerate(PLACES):
        owner = dev(*place)[0]
        left = normed[:, pl.ds(pl.multiple_of(owner * part, part), part)]
        both = dot(left, dp[...], "tn").astype(BF16)
        for i in range(2):
            g[i, owner] = both[:, i * half : (i + 1) * half]
        spread.ready(*place)
        if n == 2:
            wait_head()
            gains = in_order(eh)
            for i in range(SIDE):
                e1[i, :ng, :] = gains
            more, wait_y = share_start(e1, ey, y, lambda d: dev(0, d), se.at[1], re.at[1], SIDE, True)
            small += more
        if n == 9:
            wait_y()
            total = in_order(ey)
            for j in range(SIDE):
                e2[j, : ng + nc, :] = total[: ng + nc]
                e2[j, ng + nc :, :] = total[ng + nc + j * PAD : ng + nc + (j + 1) * PAD]
            more, wait_z = share_start(e2, ez, z, lambda d: dev(d, 0), se.at[2], re.at[2], SIDE, True)
            small += more
    feed_two = ChipSum(feed, feed_one, ta, pa, ga, ma, sa, ra)

    load_w.wait()
    low = rows // CHIPS
    hp = head_place()[3]
    dn_one = {}
    for d in FAR:
        chip = hp(d)[1] // 2
        here = pl.ds(pl.multiple_of(chip * low, low), low)
        dn[here, :] = (dot(dp[here, :], wv[...], "nt") + dot(d_rate[here, :], rate_w[...], "nt")).astype(BF16)
        dn_one.update(pair_sends(dn, pb, sb, rb, (d,)))
        spread.relays(FAR.index(d))
    feed_two.relay()
    dn_two = ChipSum(dn, dn_one, tb, pb, gb, mb, sb, rb)
    wait_z()
    total = in_order(ez)
    for r in range(n_row):
        g_feed_o[:, r * LANES : (r + 1) * LANES] = total[r : r + 1]
    for r in range(h_row):
        g_head_o[:, r * LANES : (r + 1) * LANES] = total[n_row + r : n_row + r + 1]
    own = conv_o.shape[1]
    for t in range(taps):
        for h in range(own):
            for r in range(c_row // own):
                lo = ng + t * c_row + h * (c_row // own) + r
                conv_o[t, h : h + 1, r * LANES : (r + 1) * LANES] = total[lo : lo + 1]
    dlog_o[...] = total[ng + nc - PAD : ng + nc - PAD + 1, :own]
    dbias_o[...] = total[ng + nc - PAD : ng + nc - PAD + 1, own : 2 * own]
    for i in range(2):
        rate_o[i] = total[ng + nc + i * own : ng + nc + (i + 1) * own]
    dn_two.relay()
    layer_o[...] = (hidden[...] + feed_two.result()).astype(BF16)
    d_norm, d_gain = norm_back(tokens[...].astype(F32), gain[...], dn_two.result())
    d_tokens_o[...] = d_hidden[...] + d_norm

    for r in range(n_row):
        m0[r : r + 1, :] = d_gain[:, r * LANES : (r + 1) * LANES]
    more, wait_head = share_start(m0, mh, head, across, sm.at[0], rm.at[0], heads)
    small += more

    def settle_mixer(b):
        for i in range(2):
            both = spread.total(i, b)
            if b:
                mid[i, b] = both.astype(BF16)
                settle_two.send(mid.at[i, b], i, b)
            else:
                g_mixer_o[i] = both

    settle_mixer(2)
    wait_head()
    m1[...] = in_order(mh)
    more, wait_y = share_start(m1, my, y, lambda d: dev(0, d), sm.at[1], rm.at[1])
    small += more
    settle_mixer(1)
    settle_mixer(3)
    wait_y()
    m2[...] = in_order(my)
    more, wait_z = share_start(m2, mz, z, lambda d: dev(d, 0), sm.at[2], rm.at[2])
    small += more
    settle_mixer(0)
    for i, o in ((0, g_down_o), (1, g_out_o)):
        o[...] = sums[i][0].astype(F32) + settle.others(i)
    wait_z()
    total = in_order(mz)
    for r in range(n_row):
        g_gain_o[:, r * LANES : (r + 1) * LANES] = total[r : r + 1]
    for i in range(2):
        g_mixer_o[i] = g_mixer_o[i] + settle_two.others(i)
    spread.end()
    settle.end()
    settle_two.end()
    feed_two.end()
    dn_two.end()
    for s in small + [back]:
        s.wait_send()


def hand_over(*refs):
    n = (len(refs) - 2) // 2
    srcs, dsts, (held, done) = refs[:n], refs[n : 2 * n], refs[2 * n :]
    copies = [
        pltpu.make_async_copy(srcs[i], dsts[i] if i < n - 1 else held, done.at[i]) for i in range(n - 1, -1, -1)
    ]
    for s in copies:
        s.start()
    copies[0].wait()
    for i in range(held.shape[0]):
        dsts[-1][:, i, :] = held[i]
    for s in copies[1:]:
        s.wait()


def local(
    tokens, mixer_gain, mixer_weight, rate_weight, conv_weight, decay_log, decay_bias, head_gain,
    output_weight, feed_gain, gate_up_weight, down_weight, doc_starts, cotangent,
):
    own = tokens.shape[0]
    (gathered,) = reach(
        first_norm,
        [sds((own * lax.axis_size("head"), D), BF16)],
        [pltpu.VMEM((own, D), BF16)] + gather_scratch(),
        3, 32, tokens, mixer_gain.reshape(1, D),
    )
    heads = mixer_weight.shape[1]
    mixer_flat = mixer_weight.reshape(D, heads * MIXW)
    rows = gathered.shape[0]
    blocks = rows // BLK
    units = heads * blocks
    seq = lax.axis_size("seq")
    projected = jnp.dot(gathered, mixer_flat, preferred_element_type=F32)
    rate_proj = jnp.einsum("td,dgh->tgh", gathered, rate_weight, preferred_element_type=F32).reshape(rows, 2 * heads)
    convw = conv_weight.reshape(KCONV, heads * CONVW)
    info = jnp.concatenate(
        [doc_starts, jnp.stack([lax.axis_index("seq") * rows, lax.axis_index("seq")]).astype(jnp.int32)]
    )
    dlog, dbias = decay_log.reshape(1, heads), decay_bias.reshape(1, heads)
    gain = head_gain.reshape(1, DV)

    out_flat = output_weight.reshape(heads * DV, D)
    pairs = pltpu.VMEM((SIDE, heads, DK + DV, DK), BF16)
    conv, dec, inv, wu, qe, step, states, head_out, gated, ga, ta, halo, mixed, cot_rows = reach(
        mixer_forward,
        [
            sds((rows, heads * CONVW)), sds((units, BLK, BLK)), sds((units, BLK, BLK), BF16),
            sds((units, BLK, DK + DV)), sds((rows, heads * DK)), sds((units, DK + DV, DK)), sds((units, DV, DK)),
            sds((rows, heads * DV)), sds((rows, heads * DV), BF16), sds((SIDE, heads, DK, DK), BF16),
            sds((SIDE, heads, DK, DK), BF16), sds((PAD, heads * CONVW)), sds((rows, D), BF16), sds((rows, D), BF16),
        ],
        [
            pltpu.VMEM((PAD + rows, CONVW), F32), pltpu.VMEM((rows, heads * DV), F32),
            pltpu.VMEM((rows, heads * DV), F32), pltpu.VMEM((units, BLK, BLK), BF16),
            pltpu.VMEM((heads, DK + DV, DK), BF16), pltpu.VMEM((PAD, heads * CONVW), F32),
            pltpu.VMEM((PAD, heads * CONVW), F32), pairs, pltpu.VMEM((heads, DK + DV, DK), BF16), pairs,
            pltpu.SemaphoreType.DMA, pltpu.SemaphoreType.DMA, sems(SIDE), sems(SIDE), sems(SIDE), sems(SIDE),
        ]
        + gather_scratch(),
        1, 56, info, projected, rate_proj, convw, dlog, dbias, out_flat, gain, cotangent, scalars=(0,), nbytes=30_000_000,
    )
    hid = down_weight.shape[0]
    part, half, n_head = D // seq, MIXW, lax.axis_size("head")
    gu_t = gate_up_weight.transpose(1, 2, 0).reshape(2 * hid, D)

    def sums_of_head():
        return [pltpu.VMEM((own, D), F32)] + [pltpu.VMEM((CHIPS, own, D), BF16) for _ in range(3)]

    hidden, d_mixed, d_hidden, g_feed_gain, grads, middle, feed = reach(
        feed_forward,
        [
            sds((own, D)), sds((rows, D), BF16), sds((own, D)), sds((1, D)), sds((2, SIDE, hid, LANES), BF16),
            sds((hid, rows), BF16), sds((rows, D), BF16),
        ],
        [
            pltpu.VMEM((rows, D), BF16), pltpu.VMEM((2 * hid, D), BF16), pltpu.VMEM((hid, D), BF16),
            pltpu.VMEM((hid, rows), F32), pltpu.VMEM((2 * hid, rows), BF16), pltpu.VMEM((rows, D), BF16),
            pltpu.VMEM((own, D), BF16),
        ]
        + sums_of_head()
        + sums_of_head()
        + [
            pltpu.VMEM((seq, 2, hid, LANES), BF16), pltpu.VMEM((2, SIDE, hid, LANES), BF16),
            pltpu.VMEM((2, 2, SIDE, hid, LANES), BF16), sems(2), sems(10), sems(10), sems(10), sems(10),
        ]
        + gather_scratch()
        + gather_scratch()
        + [sems(2 * SIDE * SIDE), sems(2 * SIDE * SIDE)],
        2, 63, mixed, tokens, feed_gain.reshape(1, D), cotangent, cot_rows, gu_t, down_weight,
        anywhere=(5, 6), nbytes=40_000_000,
    )
    gated_t = gated.T
    d_projected, d_tail, d_edge, d_rate, d_convw, d_decay, g_head_gain, s_down, s_out, grad_gate_up = reach(
        mixer_back,
        [
            sds((rows, heads * MIXW), BF16), sds((2 * PAD, heads * CONVW)), sds((PAD, heads * CONVW)),
            sds((rows, LANES), BF16), sds((KCONV, heads * CONVW)), sds((1, LANES)), sds((1, DV)),
            sds((SIDE, hid, LANES), BF16), sds((SIDE, heads * DV, LANES), BF16), sds((2, hid, LANES)),
        ],
        [
            pltpu.VMEM((rows, heads * DV), F32), pltpu.VMEM((units, DV, DK), F32),
            pltpu.VMEM((heads, DV, DK), BF16), pltpu.VMEM((heads, DV, DK), F32),
            pltpu.VMEM((SIDE, heads, DV, DK), BF16), pltpu.VMEM((heads, DV, DK), BF16),
            pltpu.VMEM((SIDE, heads, DV, DK), BF16),
            pltpu.VMEM((PAD + rows, CONVW), F32), pltpu.VMEM((PAD + rows, CONVW), F32),
            pltpu.VMEM((units, DV, DK), F32), pltpu.VMEM((rows, DK), F32), pltpu.VMEM((rows, heads * CONVW), F32),
            pltpu.VMEM((seq, hid, LANES), BF16), pltpu.VMEM((seq, heads * DV, LANES), BF16),
            pltpu.VMEM((SIDE, hid, LANES), BF16), pltpu.VMEM((SIDE, heads * DV, LANES), BF16),
            pltpu.VMEM((2, SIDE, hid, LANES), BF16), pltpu.VMEM((2, SIDE, heads * DV, LANES), BF16),
            pltpu.VMEM((2, SIDE, hid, LANES), BF16),
            sems(SIDE), sems(SIDE), sems(SIDE), sems(SIDE), sems(2 * SIDE * SIDE), sems(2 * SIDE * SIDE),
            sems(2 * SIDE), sems(2 * SIDE),
        ],
        4, 63, info, d_mixed, out_flat, head_out, projected, gain, qe, step, ga, ta, middle, cot_rows, gated_t, grads,
        conv, dec, inv, wu, states, rate_proj, halo, convw, dlog, dbias, scalars=(0,), nbytes=40_000_000,
    )
    rate_pad = jnp.pad(rate_weight.reshape(D, 2 * heads), ((0, 0), (0, LANES - 2 * heads)))
    n_gain, n_conv, n_last = D // LANES + PAD, KCONV * heads * CONVW // LANES + PAD, D // LANES
    n_y, n_z = n_gain + n_conv + SIDE * PAD, n_gain + n_conv + PAD

    def rows_of(*shape):
        return pltpu.VMEM(shape + (LANES,), F32)

    (
        layer_out, grad_tokens, grad_mixer, grad_mixer_gain, grad_feed_gain, grad_head_gain, grad_conv, grad_decay_log,
        grad_decay_bias, grad_rate, grad_down, grad_output,
    ) = reach(
        finish,
        [
            sds((own, D), BF16), sds((own, D)), sds((2, part, half)), sds((1, D)), sds((1, D)), sds((1, DV)),
            sds((KCONV, heads, CONVW)), sds((1, heads)), sds((1, heads)), sds((2, heads, LANES)), sds((hid, LANES)),
            sds((heads * DV, LANES)),
        ],
        [
            pltpu.VMEM((rows, heads * MIXW), BF16), pltpu.VMEM((D, heads * MIXW), BF16),
            pltpu.VMEM((PAD, heads * CONVW), F32), pltpu.VMEM((2, seq, part, half), BF16),
            pltpu.VMEM((2, SIDE, part, half), BF16), pltpu.VMEM((2, 2, SIDE, part, half), BF16),
            pltpu.VMEM((2, SIDE, part, half), BF16), pltpu.VMEM((2, SIDE, part, half), BF16), pltpu.VMEM((rows, D), BF16),
        ]
        + sums_of_head()
        + sums_of_head()
        + [
            pltpu.VMEM((SIDE, hid, LANES), BF16), pltpu.VMEM((SIDE, heads * DV, LANES), BF16),
            rows_of(n_gain), rows_of(n_head, n_gain), rows_of(SIDE, n_y), rows_of(SIDE, n_y), rows_of(SIDE, n_z),
            rows_of(SIDE, n_z), rows_of(n_last), rows_of(n_head, n_last), rows_of(n_last), rows_of(SIDE, n_last),
            rows_of(n_last), rows_of(SIDE, n_last),
            pltpu.SemaphoreType.DMA, pltpu.SemaphoreType.DMA, sems(2),
            sems(2 * SIDE * SIDE), sems(2 * SIDE * SIDE), sems(2 * SIDE), sems(2 * SIDE),
            sems(10), sems(10), sems(10), sems(10), sems(2 * SIDE), sems(2 * SIDE),
            pltpu.SemaphoreType.DMA((3, n_head)), pltpu.SemaphoreType.DMA((3, n_head)),
            pltpu.SemaphoreType.DMA((3, n_head)), pltpu.SemaphoreType.DMA((3, n_head)),
        ],
        5, 62, d_projected, gathered, mixer_flat, d_rate, rate_pad, d_tail, d_edge, feed, hidden, tokens,
        d_hidden, mixer_gain.reshape(1, D), d_convw, d_decay, g_feed_gain, g_head_gain, s_down, s_out,
        anywhere=(0, 2), nbytes=40_000_000,
    )
    results = [
        layer_out, grad_tokens, grad_mixer_gain, grad_feed_gain, grad_head_gain, grad_conv, grad_decay_log,
        grad_decay_bias, grad_rate, grad_down, grad_output, grad_gate_up, grad_mixer,
    ]
    (
        layer_out, grad_tokens, grad_mixer_gain, grad_feed_gain, grad_head_gain, grad_conv, grad_decay_log,
        grad_decay_bias, grad_rate, grad_down, grad_output, grad_gate_up, grad_mixer,
    ) = pl.pallas_call(
        hand_over,
        out_shape=[sds(v.shape, v.dtype) for v in results[:-1]] + [sds((part, heads, half))],
        in_specs=[pl.BlockSpec(memory_space=pl.ANY) for _ in results],
        out_specs=[pl.BlockSpec(memory_space=pl.ANY) for _ in results[:-1]] + [VMEM],
        scratch_shapes=[pltpu.VMEM((heads, part, half), F32), sems(len(results))],
        compiler_params=pltpu.CompilerParams(vmem_limit_bytes=60 << 20),
        cost_estimate=pl.CostEstimate(flops=0, bytes_accessed=6_000_000, transcendentals=0),
    )(*results)
    grad_gate_up = grad_gate_up.transpose(2, 0, 1)
    grad_output = grad_output.reshape(heads, DV, LANES)
    grad_rate = grad_rate.transpose(2, 0, 1)
    grad_mixer_gain, grad_feed_gain, grad_head_gain = (
        v.reshape(-1) for v in (grad_mixer_gain, grad_feed_gain, grad_head_gain)
    )
    grad_decay_log, grad_decay_bias = grad_decay_log.reshape(-1), grad_decay_bias.reshape(-1)
    return (
        layer_out, grad_tokens, grad_mixer_gain, grad_mixer, grad_rate, grad_conv, grad_decay_log, grad_decay_bias,
        grad_head_gain, grad_output, grad_feed_gain, grad_gate_up, grad_down,
    )


def solution(mesh):
    rows = P(("seq", "head"), None)
    return jax.shard_map(
        local,
        mesh=mesh,
        in_specs=(
            rows, P(), P(None, "head", None), P(None, None, "head"), P(None, "head", None), P("head"), P("head"),
            P(), P("head", None, None), P(), P(None, None, "head"), P("head", None), P(), rows,
        ),
        out_specs=(
            rows, rows, P(), P("seq", "head", None), P("seq", None, "head"), P(None, "head", None), P("head"),
            P("head"), P(), P("head", None, "seq"), P(), P("seq", None, "head"), P("head", "seq"),
        ),
        check_vma=False,
    )
```

profile of v0, /device:TPU:1, one launch (start us, length us, event | category | flops | bytes accessed | tf_op | source)
XLA Modules:
  0.0 356.0 jit_solution(12422518799992583895)
XLA Ops:
  0.6 0.0 copy-start.1
  0.7 0.9 copy-done.1
  1.6 0.0 copy-start.2
  1.6 0.7 copy-done.2
  2.3 16.7 %shard_map.237.normed = bf16[512,2048]{1,0:T(8,128)(2,1)S(1)} custom-call(bf16[64,2048]{1,0:T(8,128)(2,1)S(1)} %copy-done.1, f32[1,2048]{1,0:T(1,128)S(1)} %bitcast.35), custom_call_target="tpu_custom_call" | custom-call | bytes 12000000 | tf_op jit(solution)/shard_map/pallas_call | solution.py:627
  19.0 0.0 copy-start
  19.0 4.9 %copy.34 = bf16[256,8,2,768]{3,1,2,0:T(8,128)(2,1)S(1)} copy(bf16[256,8,2,768]{3,2,1,0:T(2,128)(2,1)} %bitcast.40) | data formatting | bytes 12582912
  24.0 0.0 copy-start.3
  24.0 0.0 copy-start.5
  24.0 5.1 %fusion.2.proj = f32[512,1536]{1,0:T(8,128)} fusion(bf16[512,2048]{1,0:T(8,128)(2,1)S(1)} %shard_map.237.normed, bf16[2048,1536]{1,0:T(8,128)(2,1)S(1)} %bitcast.36), kind=kOutput, calls=%fused_computation.3 | convolution fusion | flops 3221225472 | bytes 11534336 | tf_op jit(solution)/shard_map/dot_general | solution.py:1093
  29.1 0.0 copy-done
  29.1 0.0 copy-done.3
  29.1 0.0 copy-done.5
  29.1 0.0 copy-start.7
  29.1 0.0 copy-start.6
  29.1 0.6 fusion
  29.8 0.9 copy.30.rate
  30.7 0.0 copy-done.7
  30.7 0.6 pad_add_fusion.info
  31.3 0.0 copy-done.6
  31.3 0.6 copy.35
  31.9 61.5 %shard_map.238 = (f32[512,1024]{1,0:T(8,128)}, f32[4,256,256]{2,1,0:T(8,128)}, bf16[4,256,256]{2,1,0:T(8,128)(2,1)}, f32[4,256,384]{2,1,0:T(8,128)}, f32[512,256...) custom-call(s32[6]{0:T(128)} %pad_add_fusion.info, ...), custom_call_target="tpu_custom_call" | custom-call | bytes 30000000 | tf_op jit(solution)/shard_map/pallas_call | solution.py:627
  93.4 0.0 copy-start.4
  93.4 70.9 %shard_map.239 = (f32[64,2048]{1,0:T(8,128)}, bf16[512,2048]{1,0:T(8,128)(2,1)}, f32[64,2048]{1,0:T(8,128)}, f32[1,2048]{1,0:T(1,128)}, bf16[2,4,688,128]{3,2,1,...) custom-call(bf16[512,2048]{1,0:T(8,128)(2,1)} %get-tuple-element.69.x, bf16[64,2048]{1,0:T(8,128)(2,1)} %tokens.5, ...), custom_call_target="tpu_custom_call" | custom-call | bytes 40000000 | tf_op jit(solution)/shard_map/pallas_call | solution.py:627
  164.3 0.0 copy-done.4
  164.3 1.0 copy.31
  165.3 56.1 %shard_map.240 = (bf16[512,1536]{1,0:T(8,128)(2,1)}, f32[16,1024]{1,0:T(8,128)}, f32[8,1024]{1,0:T(8,128)}, bf16[512,128]{1,0:T(8,128)(2,1)}, f32[4,1024]{1,0:T(...) custom-call(s32[6]{0:T(128)} %pad_add_fusion.info, ...), custom_call_target="tpu_custom_call" | custom-call | bytes 40000000 | tf_op jit(solution)/shard_map/pallas_call | solution.py:627
  221.5 0.3 copy.33
  221.8 0.9 pad.4.rate_w
  222.7 66.1 %shard_map.241 = (bf16[64,2048]{1,0:T(8,128)(2,1)}, f32[64,2048]{1,0:T(8,128)}, f32[2,128,768]{2,1,0:T(8,128)}, f32[1,2048]{1,0:T(1,128)}, f32[1,2048]{1,0:T(1,1...) custom-call(bf16[512,1536]{1,0:T(8,128)(2,1)} %get-tuple-element.86., ...), custom_call_target="tpu_custom_call" | custom-call | bytes 40000000 | tf_op jit(solution)/shard_map/pallas_call | solution.py:627
  288.8 67.0 %shard_map.242 = (bf16[64,2048]{1,0:T(8,128)(2,1)}, f32[64,2048]{1,0:T(8,128)}, f32[1,2048]{1,0:T(1,128)}, f32[1,2048]{1,0:T(1,128)}, f32[1,256]{1,0:T(1,128)}, ...) custom-call(bf16[64,2048]{1,0:T(8,128)(2,1)} %get-tuple-element.99.r, ...), custom_call_target="tpu_custom_call" | custom-call | bytes 6000000 | tf_op jit(solution)/shard_map/pallas_call | solution.py:1224
  (2 shorter events, 0.0 us)
Async XLA Ops:
  0.6 1.0 copy-start.1
  1.6 0.7 copy-start.2
  19.0 10.1 %copy-start = (bf16[512,2048]{1,0:T(8,128)(2,1)}, bf16[512,2048]{1,0:T(8,128)(2,1)S(1)}, u32[]{:S(2)}) copy-start(bf16[512,2048]{1,0:T(8,128)(2,1)S(1)} %shard_map.237.normed) | copy-start | bytes 6291460
  24.0 5.1 %copy-start.3 = (bf16[256,8,2,768]{3,1,2,0:T(8,128)(2,1)}, bf16[256,8,2,768]{3,1,2,0:T(8,128)(2,1)S(1)}, u32[]{:S(2)}) copy-start(bf16[256,8,2,768]{3,1,2,0:T(8,128)(2,1)S(1)} %copy.34) | copy-start | bytes 18874372
  24.0 5.1 %copy-start.5 = (bf16[2048,2,2]{0,2,1:T(2,128)(2,1)S(1)}, bf16[2048,2,2]{0,2,1:T(2,128)(2,1)}, u32[]{:S(2)}) copy-start(bf16[2048,2,2]{0,2,1:T(2,128)(2,1)} %param.17) | copy-start | bytes 49156
  29.1 1.6 copy-start.7
  29.1 2.1 copy-start.6
  93.4 70.9 %copy-start.4 = (bf16[512,512]{1,0:T(8,128)(2,1)S(1)}, bf16[512,512]{1,0:T(8,128)(2,1)}, u32[]{:S(2)}) copy-start(bf16[512,512]{1,0:T(8,128)(2,1)} %get-tuple-element.78) | copy-start | bytes 1572868
where the time goes:
time: 360 us; the launch traced here: 356 us
  Pallas kernels  338 us (94%)
  local copies, waits for them, and re-layouts  10.3 us (3%)
  matrix products  5.76 us (2%)
    pallas_call x5, Pallas kernels, reach(): pl.pallas_call(kernel, out_shape=outs, in_specs=[pl.BlockSpec(memory_spac...  271 us
    pallas_call x1, Pallas kernels, local(): pl.pallas_call(hand_over, out_shape=[sds(v.shape, v.dtype) for v in resul...  67 us

commit v1 on v0

--- a/solution.py
+++ b/solution.py
@@ -281,6 +281,7 @@
     rate, halo, convw, dlog, dbias,
     d_proj_o, d_tail_o, d_edge_o, d_rate_o, d_convw_o, d_decay_o, d_gain_o, s_down_o, s_out_o, g_gu_o,
     d_out, y, inc, later, got1, tot, got2, xpad, dpad, dsend, cols_s, d_pre_o,
+    gm_s, e_s, fresh_s, ks_s, d_fresh_s, dq_s, dk_s, cols_u,
     g_down, g_out, relay_d, relay_o, got_d, got_o, last_got, s1, r1, s2, r2, s3, r3, s4, r4
 ):
     greet(side_peers())
@@ -295,27 +296,58 @@
     )
     d_gain_o[...] = head_back(d_mixed, out_w, head_out, proj, gain, qe, step, d_out, d_proj_o, y, inc)
 
-    def make(o, left, right):
-        for j in range(0, o.shape[0], 2):
-            both = dot(left[...], right[:, j * LANES : (j + 2) * LANES]).astype(BF16)
-            o[j], o[j + 1] = both[:, :LANES], both[:, LANES:]
-
-    def level_one():
-        make(g_down, middle, cot)
-        make(g_out, gated_t, d_mixed)
-
-    def level_two():
-        for place in PLACES:
-            spread.ready(*place, (0,))
-
-    swaps = states_backward(inc, ga, ta, later, got1, tot, got2, s1, r1, s2, r2, level_one, level_two)
-    for place in PLACES:
-        spread.ready(*place, (1,))
     rows = d_out.shape[0]
     heads = later.shape[0]
     blocks = rows // BLK
     strength, log_decay, pre = rates(rate, dlog, dbias)
     valid = [valid_column(info, rows, KCONV - 1 - j) for j in range(KCONV)]
+
+    def early(c):
+        keep, first, last, tri, strict = block_masks(info, c)
+        here = pl.ds(c * BLK, BLK)
+        for h in range(heads):
+            u = h * blocks + c
+            qa, ka, va, rq, rk = vectors(conv[here, pl.ds(h * CONVW, CONVW)])
+            q, k = qa * (rq * DK**-0.5), ka * rk
+            g = log_decay[c * BLK : (c + 1) * BLK, h : h + 1]
+            carry, to_end = decays(g, first, last, tri)
+            dm = dec[u]
+            sc = dm * dot3(q, k, "nt")
+            gm_s[u] = dm * dot3(k, k, "nt") * strict
+            state = states[u]
+            do = d_out[here, pl.ds(h * DV, DV)]
+            ks_s[u] = dot3(k, state, "nt")
+            fresh = wu[u, :, DK:] - dot3(wu[u, :, :DK], state, "nt")
+            fresh_s[u] = fresh
+            d_fresh_s[u] = dot(sc, do, "tn")
+            d_sc = dot3(do, fresh, "nt")
+            e_s[u] = d_sc * sc
+            d_scd = d_sc * dm
+            dq_s[u] = dot(d_scd, k) + carry * dot(do, state)
+            dk_s[u] = dot(d_scd, q, "tn")
+            cols_u[u, :, 0:1] = carry
+            cols_u[u, :, 1:2] = to_end
+            cols_u[u, :, 2:3] = jnp.sum(do * dot3(q, state, "nt"), axis=1, keepdims=True)
+
+    def make(o, left, right):
+        for j in range(0, o.shape[0], 2):
+            both = dot(left[...], right[:, j * LANES : (j + 2) * LANES]).astype(BF16)
+            o[j], o[j + 1] = both[:, :LANES], both[:, LANES:]
+
+    def level_one():
+        make(g_down, middle, cot)
+        make(g_out, gated_t, d_mixed)
+        early(0)
+
+    def level_two():
+        for place in PLACES:
+            spread.ready(*place, (0,))
+        for c in range(1, blocks):
+            early(c)
+
+    swaps = states_backward(inc, ga, ta, later, got1, tot, got2, s1, r1, s2, r2, level_one, level_two)
+    for place in PLACES:
+        spread.ready(*place, (1,))
     for h in range(heads):
         grad = later[h]
         for c in range(blocks - 1, -1, -1):
@@ -324,7 +356,7 @@
             if c:
                 grad = dot3(grad, step[u, :DK, :], "nt") + y[u]
     for c in range(blocks):
-        keep, first, last, tri, strict = block_masks(info, c)
+        tri, strict = block_masks(info, c)[3:]
         here = pl.ds(c * BLK, BLK)
         for h in range(heads):
             u = h * blocks + c
@@ -332,40 +364,31 @@
             sg = sigmoid(cv)
             qa, ka, va, rq, rk = vectors(cv)
             rqs = rq * DK**-0.5
-            q, k = qa * rqs, ka * rk
+            k = ka * rk
             beta = strength[c * BLK : (c + 1) * BLK, h : h + 1]
-            g = log_decay[c * BLK : (c + 1) * BLK, h : h + 1]
-            carry, to_end = decays(g, first, last, tri)
+            carry, to_end, hq = cols_u[u, :, 0:1], cols_u[u, :, 1:2], cols_u[u, :, 2:3]
             dm = dec[u]
-            sc = dm * dot3(q, k, "nt")
-            gm = dm * dot3(k, k, "nt") * strict
+            gm, fresh, ks = gm_s[u], fresh_s[u], ks_s[u]
             state, d_end = states[u], dsend[u]
-            do = d_out[here, pl.ds(h * DV, DV)]
-            ks = dot3(k, state, "nt")
-            qs = dot3(q, state, "nt")
-            fresh = wu[u, :, DK:] - dot3(wu[u, :, :DK], state, "nt")
             kd = to_end * k
-            d_fresh = dot(sc, do, "tn") + dot(kd, d_end, "nt")
-            ah, al = halves(d_fresh)
+            ah, al = halves(d_fresh_s[u] + dot(kd, d_end, "nt"))
             d_rhs = dot(inv[u], ah, "tn") + dot(inv[u], al, "tn")
             d_low = -dot3(d_rhs, fresh, "nt")
-            d_sc = dot3(do, fresh, "nt")
             d_val = beta * d_rhs
             ebar = d_low * gm
             d_beta = jnp.sum(d_rhs * (va - carry * ks), axis=1, keepdims=True) + jnp.sum(ebar, axis=1, keepdims=True)
-            e = d_sc * sc + beta * ebar
-            d_scd = d_sc * dm
+            e = e_s[u] + beta * ebar
             d_gm = (beta * d_low) * (dm * strict)
             d_kd = dot(fresh, d_end)
-            d_q = dot(d_scd, k) + carry * dot(do, state)
+            d_q = dq_s[u]
             d_k = (
-                dot(d_scd, q, "tn")
+                dk_s[u]
                 - (beta * carry) * dot(d_rhs, state)
                 + to_end * d_kd
                 + dot(d_gm, k)
                 + dot(d_gm, k, "tn")
             )
-            hcol = carry * jnp.sum(do * qs - beta * d_rhs * ks, axis=1, keepdims=True)
+            hcol = carry * (hq - jnp.sum(beta * d_rhs * ks, axis=1, keepdims=True))
             fcol = jnp.sum(kd * d_kd, axis=1, keepdims=True)
             tail = carry[BLK - 1 :, :] * jnp.sum(
                 jnp.sum(state * d_end, axis=1, keepdims=True), axis=0, keepdims=True
@@ -1164,6 +1187,9 @@
             pltpu.VMEM((SIDE, heads, DV, DK), BF16),
             pltpu.VMEM((PAD + rows, CONVW), F32), pltpu.VMEM((PAD + rows, CONVW), F32),
             pltpu.VMEM((units, DV, DK), F32), pltpu.VMEM((rows, DK), F32), pltpu.VMEM((rows, heads * CONVW), F32),
+            pltpu.VMEM((units, BLK, BLK), F32), pltpu.VMEM((units, BLK, BLK), F32), pltpu.VMEM((units, BLK, DV), F32),
+            pltpu.VMEM((units, BLK, DV), F32), pltpu.VMEM((units, BLK, DV), F32), pltpu.VMEM((units, BLK, DK), F32),
+            pltpu.VMEM((units, BLK, DK), F32), pltpu.VMEM((units, BLK, LANES), F32),
             pltpu.VMEM((seq, hid, LANES), BF16), pltpu.VMEM((seq, heads * DV, LANES), BF16),
             pltpu.VMEM((SIDE, hid, LANES), BF16), pltpu.VMEM((SIDE, heads * DV, LANES), BF16),
             pltpu.VMEM((2, SIDE, hid, LANES), BF16), pltpu.VMEM((2, SIDE, heads * DV, LANES), BF16),
@@ -1225,7 +1251,7 @@
         hand_over,
         out_shape=[sds(v.shape, v.dtype) for v in results[:-1]] + [sds((part, heads, half))],
         in_specs=[pl.BlockSpec(memory_space=pl.ANY) for _ in results],
-        out_specs=[pl.BlockSpec(memory_space=pl.ANY) for _ in results[:-1]] + [VMEM],
+        out_specs=[VMEM for _ in results],
         scratch_shapes=[pltpu.VMEM((heads, part, half), F32), sems(len(results))],
         compiler_params=pltpu.CompilerParams(vmem_limit_bytes=60 << 20),
         cost_estimate=pl.CostEstimate(flops=0, bytes_accessed=6_000_000, transcendentals=0),

time: 360 us -> 297 us (0.82)
  Pallas kernels: 338 us -> 275 us
    pallas_call x1, Pallas kernels: 67 us -> 3.51 us  [local(): pl.pallas_call(hand_over, out_shape=[sds(v.shape, v.dtype) for v in resul...]
where the time goes in v1:
time: 297 us; the launch traced here: 293 us
  Pallas kernels  275 us (93%)
  local copies, waits for them, and re-layouts  10.3 us (3%)
  matrix products  5.76 us (2%)
    pallas_call x5, Pallas kernels, reach(): pl.pallas_call(kernel, out_shape=outs, in_specs=[pl.BlockSpec(memory_spac...  272 us
    unnamed x18, local copies, waits for them, and re-layouts  7.17 us

profile of v1, /device:TPU:1, one launch (start us, length us, event | category | flops | bytes accessed | tf_op | source)
XLA Modules:
  0.0 292.8 jit_solution(10607612450180443055)
XLA Ops:
  0.6 0.0 copy-start.1
  0.7 0.9 copy-done.1
  1.6 0.0 copy-start.2
  1.6 0.7 copy-done.2
  2.3 16.7 %shard_map.237.normed = bf16[512,2048]{1,0:T(8,128)(2,1)S(1)} custom-call(bf16[64,2048]{1,0:T(8,128)(2,1)S(1)} %copy-done.1, f32[1,2048]{1,0:T(1,128)S(1)} %bitcast.35), custom_call_target="tpu_custom_call" | custom-call | bytes 12000000 | tf_op jit(solution)/shard_map/pallas_call | solution.py:650
  19.0 0.0 copy-start
  19.0 4.9 %copy.34 = bf16[256,8,2,768]{3,1,2,0:T(8,128)(2,1)S(1)} copy(bf16[256,8,2,768]{3,2,1,0:T(2,128)(2,1)} %bitcast.40) | data formatting | bytes 12582912
  24.0 0.0 copy-start.3
  24.0 0.0 copy-start.5
  24.0 5.1 %fusion.2.proj = f32[512,1536]{1,0:T(8,128)} fusion(bf16[512,2048]{1,0:T(8,128)(2,1)S(1)} %shard_map.237.normed, bf16[2048,1536]{1,0:T(8,128)(2,1)S(1)} %bitcast.36), kind=kOutput, calls=%fused_computation.3 | convolution fusion | flops 3221225472 | bytes 11534336 | tf_op jit(solution)/shard_map/dot_general | solution.py:1116
  29.1 0.0 copy-done
  29.1 0.0 copy-done.3
  29.1 0.0 copy-done.5
  29.1 0.0 copy-start.7
  29.1 0.0 copy-start.6
  29.1 0.6 fusion
  29.8 0.9 copy.30.rate
  30.7 0.0 copy-done.7
  30.7 0.6 pad_add_fusion.info
  31.3 0.0 copy-done.6
  31.3 0.6 copy.35
  31.9 61.5 %shard_map.238 = (f32[512,1024]{1,0:T(8,128)}, f32[4,256,256]{2,1,0:T(8,128)}, bf16[4,256,256]{2,1,0:T(8,128)(2,1)}, f32[4,256,384]{2,1,0:T(8,128)}, f32[512,256...) custom-call(s32[6]{0:T(128)} %pad_add_fusion.info, ...), custom_call_target="tpu_custom_call" | custom-call | bytes 30000000 | tf_op jit(solution)/shard_map/pallas_call | solution.py:650
  93.4 0.0 copy-start.4
  93.4 70.9 %shard_map.239 = (f32[64,2048]{1,0:T(8,128)}, bf16[512,2048]{1,0:T(8,128)(2,1)}, f32[64,2048]{1,0:T(8,128)}, f32[1,2048]{1,0:T(1,128)}, bf16[2,4,688,128]{3,2,1,...) custom-call(bf16[512,2048]{1,0:T(8,128)(2,1)} %get-tuple-element.69.x, bf16[64,2048]{1,0:T(8,128)(2,1)} %tokens.5, ...), custom_call_target="tpu_custom_call" | custom-call | bytes 40000000 | tf_op jit(solution)/shard_map/pallas_call | solution.py:650
  164.3 0.0 copy-done.4
  164.3 1.0 copy.31
  165.3 55.9 %shard_map.240 = (bf16[512,1536]{1,0:T(8,128)(2,1)}, f32[16,1024]{1,0:T(8,128)}, f32[8,1024]{1,0:T(8,128)}, bf16[512,128]{1,0:T(8,128)(2,1)}, f32[4,1024]{1,0:T(...) custom-call(s32[6]{0:T(128)} %pad_add_fusion.info, ...), custom_call_target="tpu_custom_call" | custom-call | bytes 40000000 | tf_op jit(solution)/shard_map/pallas_call | solution.py:650
  221.2 0.3 copy.33
  221.5 0.9 pad.4.rate_w
  222.4 66.6 %shard_map.241 = (bf16[64,2048]{1,0:T(8,128)(2,1)}, f32[64,2048]{1,0:T(8,128)}, f32[2,128,768]{2,1,0:T(8,128)}, f32[1,2048]{1,0:T(1,128)}, f32[1,2048]{1,0:T(1,1...) custom-call(bf16[512,1536]{1,0:T(8,128)(2,1)} %get-tuple-element.86., ...), custom_call_target="tpu_custom_call" | custom-call | bytes 40000000 | tf_op jit(solution)/shard_map/pallas_call | solution.py:650
  289.0 3.5 %shard_map.242 = (bf16[64,2048]{1,0:T(8,128)(2,1)}, f32[64,2048]{1,0:T(8,128)}, f32[1,2048]{1,0:T(1,128)}, f32[1,2048]{1,0:T(1,128)}, f32[1,256]{1,0:T(1,128)}, ...) custom-call(bf16[64,2048]{1,0:T(8,128)(2,1)} %get-tuple-element.99.r, ...), custom_call_target="tpu_custom_call" | custom-call | bytes 6000000 | tf_op jit(solution)/shard_map/pallas_call | solution.py:1250
  (2 shorter events, 0.0 us)
Async XLA Ops:
  0.6 1.0 copy-start.1
  1.6 0.7 copy-start.2
  19.0 10.1 %copy-start = (bf16[512,2048]{1,0:T(8,128)(2,1)}, bf16[512,2048]{1,0:T(8,128)(2,1)S(1)}, u32[]{:S(2)}) copy-start(bf16[512,2048]{1,0:T(8,128)(2,1)S(1)} %shard_map.237.normed) | copy-start | bytes 6291460
  24.0 5.1 %copy-start.3 = (bf16[256,8,2,768]{3,1,2,0:T(8,128)(2,1)}, bf16[256,8,2,768]{3,1,2,0:T(8,128)(2,1)S(1)}, u32[]{:S(2)}) copy-start(bf16[256,8,2,768]{3,1,2,0:T(8,128)(2,1)S(1)} %copy.34) | copy-start | bytes 18874372
  24.0 5.1 %copy-start.5 = (bf16[2048,2,2]{0,2,1:T(2,128)(2,1)S(1)}, bf16[2048,2,2]{0,2,1:T(2,128)(2,1)}, u32[]{:S(2)}) copy-start(bf16[2048,2,2]{0,2,1:T(2,128)(2,1)} %param.17) | copy-start | bytes 49156
  29.1 1.6 copy-start.7
  29.1 2.1 copy-start.6
  93.4 70.9 %copy-start.4 = (bf16[512,512]{1,0:T(8,128)(2,1)S(1)}, bf16[512,512]{1,0:T(8,128)(2,1)}, u32[]{:S(2)}) copy-start(bf16[512,512]{1,0:T(8,128)(2,1)} %get-tuple-element.78) | copy-start | bytes 1572868

commit v2 on v1

--- a/solution.py
+++ b/solution.py
@@ -289,11 +289,19 @@
     for b in (2, 1, 3):
         for i in range(2):
             settle.send(s_gu.at[i, b], i, b)
-    grads = (g_down, g_out)
+    grads = (g_out, g_down)
     spread = Spread(
-        lambda i, owner: grads[i].at[owner], lambda i, b: (relay_d, relay_o)[i].at[b],
-        lambda i, s, b: (got_d, got_o)[i].at[s, b], s3, r3,
+        lambda i, owner: grads[i].at[owner], lambda i, b: (relay_o, relay_d)[i].at[b],
+        lambda i, s, b: (got_o, got_d)[i].at[s, b], s3, r3,
     )
+    def make(o, left, right):
+        for j in range(0, o.shape[0], 2):
+            both = dot(left[...], right[:, j * LANES : (j + 2) * LANES]).astype(BF16)
+            o[j], o[j + 1] = both[:, :LANES], both[:, LANES:]
+
+    make(g_down, middle, cot)
+    for place in PLACES:
+        spread.ready(*place, (1,))
     d_gain_o[...] = head_back(d_mixed, out_w, head_out, proj, gain, qe, step, d_out, d_proj_o, y, inc)
 
     rows = d_out.shape[0]
@@ -329,13 +337,7 @@
             cols_u[u, :, 1:2] = to_end
             cols_u[u, :, 2:3] = jnp.sum(do * dot3(q, state, "nt"), axis=1, keepdims=True)
 
-    def make(o, left, right):
-        for j in range(0, o.shape[0], 2):
-            both = dot(left[...], right[:, j * LANES : (j + 2) * LANES]).astype(BF16)
-            o[j], o[j + 1] = both[:, :LANES], both[:, LANES:]
-
     def level_one():
-        make(g_down, middle, cot)
         make(g_out, gated_t, d_mixed)
         early(0)
 
@@ -346,8 +348,7 @@
             early(c)
 
     swaps = states_backward(inc, ga, ta, later, got1, tot, got2, s1, r1, s2, r2, level_one, level_two)
-    for place in PLACES:
-        spread.ready(*place, (1,))
+    spread.relays(None, (1,))
     for h in range(heads):
         grad = later[h]
         for c in range(blocks - 1, -1, -1):
@@ -406,7 +407,7 @@
             d_ka = rk * d_k - ka * (rk * rk * rk * jnp.sum(d_k * ka, axis=1, keepdims=True))
             d_act = jnp.concatenate([d_qa, d_ka, d_val], axis=1)
             d_pre_o[here, pl.ds(h * CONVW, CONVW)] = d_act * (sg * (1.0 + cv * (1.0 - sg)))
-            spread.relays(c * heads + h)
+            spread.relays(c * heads + h, (0,))
     d_g, d_beta = cols_s[:, :heads], cols_s[:, heads : 2 * heads]
     d_bias = -d_g * jnp.exp(dlog[...]) * sigmoid(pre)
     rest = jnp.zeros((rows, LANES - 2 * heads), F32)
@@ -430,7 +431,7 @@
         d_proj_o[:, src] = dpad[PAD:, :].astype(BF16)
     for i in range(2):
         g_gu_o[i] = s_gu[i, 0].astype(F32) + settle.others(i)
-    for i, o in ((0, s_down_o), (1, s_out_o)):
+    for i, o in ((1, s_down_o), (0, s_out_o)):
         for b in FAR:
             o[b] = spread.total(i, b).astype(BF16)
     spread.end()
@@ -729,11 +730,11 @@
             if a and not self.late(a, b):
                 self.send(i, a, b, owner)
 
-    def relays(self, part=None):
+    def relays(self, part=None, halves_=(0, 1)):
         for n, b in enumerate(FAR):
             if part is not None and n != part:
                 continue
-            for i in range(2):
+            for i in halves_:
                 a = 1 if b in FIRST else 3
                 owner = self.way(i, a, b)[0]
                 self.copy(i, 2, b, owner).wait_recv()
@@ -964,8 +965,8 @@
             at = (j * SIDE + i) * LANES
             e1[i, ng + nc + j * PAD : ng + nc + (j + 1) * PAD, :] = rates_t[:, at : at + LANES]
 
-    sums = (s_down, s_out)
-    settle = Settle(lambda i, b: (got_d, got_o)[i].at[b], s5, r5)
+    sums = (s_out, s_down)
+    settle = Settle(lambda i, b: (got_o, got_d)[i].at[b], s5, r5)
     for b in (2, 1, 3):
         for i in range(2):
             settle.send(sums[i].at[b], i, b)
@@ -1064,7 +1065,7 @@
     more, wait_z = share_start(m2, mz, z, lambda d: dev(d, 0), sm.at[2], rm.at[2])
     small += more
     settle_mixer(0)
-    for i, o in ((0, g_down_o), (1, g_out_o)):
+    for i, o in ((1, g_down_o), (0, g_out_o)):
         o[...] = sums[i][0].astype(F32) + settle.others(i)
     wait_z()
     total = in_order(mz)

time: 297 us -> 298 us (level)
  no operation moved by 1% of the time
where the time goes in v2:
time: 298 us; the launch traced here: 294 us
  Pallas kernels  277 us (93%)
  local copies, waits for them, and re-layouts  10.3 us (3%)
  matrix products  5.76 us (2%)
    pallas_call x5, Pallas kernels, reach(): pl.pallas_call(kernel, out_shape=outs, in_specs=[pl.BlockSpec(memory_spac...  273 us
    unnamed x18, local copies, waits for them, and re-layouts  7.17 us

profile of v2, /device:TPU:1, one launch (start us, length us, event | category | flops | bytes accessed | tf_op | source)
XLA Modules:
  0.0 294.3 jit_solution(17530526617283906576)
XLA Ops:
  0.6 0.0 copy-start.1
  0.7 0.9 copy-done.1
  1.6 0.0 copy-start.2
  1.6 0.7 copy-done.2
  2.3 16.7 %shard_map.237.normed = bf16[512,2048]{1,0:T(8,128)(2,1)S(1)} custom-call(bf16[64,2048]{1,0:T(8,128)(2,1)S(1)} %copy-done.1, f32[1,2048]{1,0:T(1,128)S(1)} %bitcast.35), custom_call_target="tpu_custom_call" | custom-call | bytes 12000000 | tf_op jit(solution)/shard_map/pallas_call | solution.py:651
  19.0 0.0 copy-start
  19.0 4.9 %copy.34 = bf16[256,8,2,768]{3,1,2,0:T(8,128)(2,1)S(1)} copy(bf16[256,8,2,768]{3,2,1,0:T(2,128)(2,1)} %bitcast.40) | data formatting | bytes 12582912
  24.0 0.0 copy-start.3
  24.0 0.0 copy-start.5
  24.0 5.1 %fusion.2.proj = f32[512,1536]{1,0:T(8,128)} fusion(bf16[512,2048]{1,0:T(8,128)(2,1)S(1)} %shard_map.237.normed, bf16[2048,1536]{1,0:T(8,128)(2,1)S(1)} %bitcast.36), kind=kOutput, calls=%fused_computation.3 | convolution fusion | flops 3221225472 | bytes 11534336 | tf_op jit(solution)/shard_map/dot_general | solution.py:1117
  29.1 0.0 copy-done
  29.1 0.0 copy-done.3
  29.1 0.0 copy-done.5
  29.1 0.0 copy-start.7
  29.1 0.0 copy-start.6
  29.1 0.6 fusion
  29.8 0.9 copy.30.rate
  30.7 0.0 copy-done.7
  30.7 0.6 pad_add_fusion.info
  31.3 0.0 copy-done.6
  31.3 0.6 copy.35
  31.9 61.5 %shard_map.238 = (f32[512,1024]{1,0:T(8,128)}, f32[4,256,256]{2,1,0:T(8,128)}, bf16[4,256,256]{2,1,0:T(8,128)(2,1)}, f32[4,256,384]{2,1,0:T(8,128)}, f32[512,256...) custom-call(s32[6]{0:T(128)} %pad_add_fusion.info, ...), custom_call_target="tpu_custom_call" | custom-call | bytes 30000000 | tf_op jit(solution)/shard_map/pallas_call | solution.py:651
  93.4 0.0 copy-start.4
  93.4 70.9 %shard_map.239 = (f32[64,2048]{1,0:T(8,128)}, bf16[512,2048]{1,0:T(8,128)(2,1)}, f32[64,2048]{1,0:T(8,128)}, f32[1,2048]{1,0:T(1,128)}, bf16[2,4,688,128]{3,2,1,...) custom-call(bf16[512,2048]{1,0:T(8,128)(2,1)} %get-tuple-element.69.x, bf16[64,2048]{1,0:T(8,128)(2,1)} %tokens.5, ...), custom_call_target="tpu_custom_call" | custom-call | bytes 40000000 | tf_op jit(solution)/shard_map/pallas_call | solution.py:651
  164.3 0.0 copy-done.4
  164.3 1.0 copy.31
  165.3 55.8 %shard_map.240 = (bf16[512,1536]{1,0:T(8,128)(2,1)}, f32[16,1024]{1,0:T(8,128)}, f32[8,1024]{1,0:T(8,128)}, bf16[512,128]{1,0:T(8,128)(2,1)}, f32[4,1024]{1,0:T(...) custom-call(s32[6]{0:T(128)} %pad_add_fusion.info, ...), custom_call_target="tpu_custom_call" | custom-call | bytes 40000000 | tf_op jit(solution)/shard_map/pallas_call | solution.py:651
  221.1 0.3 copy.33
  221.4 0.9 pad.4.rate_w
  222.3 68.2 %shard_map.241 = (bf16[64,2048]{1,0:T(8,128)(2,1)}, f32[64,2048]{1,0:T(8,128)}, f32[2,128,768]{2,1,0:T(8,128)}, f32[1,2048]{1,0:T(1,128)}, f32[1,2048]{1,0:T(1,1...) custom-call(bf16[512,1536]{1,0:T(8,128)(2,1)} %get-tuple-element.86., ...), custom_call_target="tpu_custom_call" | custom-call | bytes 40000000 | tf_op jit(solution)/shard_map/pallas_call | solution.py:651
  290.5 3.5 %shard_map.242 = (bf16[64,2048]{1,0:T(8,128)(2,1)}, f32[64,2048]{1,0:T(8,128)}, f32[1,2048]{1,0:T(1,128)}, f32[1,2048]{1,0:T(1,128)}, f32[1,256]{1,0:T(1,128)}, ...) custom-call(bf16[64,2048]{1,0:T(8,128)(2,1)} %get-tuple-element.99.r, ...), custom_call_target="tpu_custom_call" | custom-call | bytes 6000000 | tf_op jit(solution)/shard_map/pallas_call | solution.py:1251
  (2 shorter events, 0.0 us)
Async XLA Ops:
  0.6 1.0 copy-start.1
  1.6 0.7 copy-start.2
  19.0 10.1 %copy-start = (bf16[512,2048]{1,0:T(8,128)(2,1)}, bf16[512,2048]{1,0:T(8,128)(2,1)S(1)}, u32[]{:S(2)}) copy-start(bf16[512,2048]{1,0:T(8,128)(2,1)S(1)} %shard_map.237.normed) | copy-start | bytes 6291460
  24.0 5.1 %copy-start.3 = (bf16[256,8,2,768]{3,1,2,0:T(8,128)(2,1)}, bf16[256,8,2,768]{3,1,2,0:T(8,128)(2,1)S(1)}, u32[]{:S(2)}) copy-start(bf16[256,8,2,768]{3,1,2,0:T(8,128)(2,1)S(1)} %copy.34) | copy-start | bytes 18874372
  24.0 5.1 %copy-start.5 = (bf16[2048,2,2]{0,2,1:T(2,128)(2,1)S(1)}, bf16[2048,2,2]{0,2,1:T(2,128)(2,1)}, u32[]{:S(2)}) copy-start(bf16[2048,2,2]{0,2,1:T(2,128)(2,1)} %param.17) | copy-start | bytes 49156
  29.1 1.6 copy-start.7
  29.1 2.1 copy-start.6
  93.4 70.9 %copy-start.4 = (bf16[512,512]{1,0:T(8,128)(2,1)S(1)}, bf16[512,512]{1,0:T(8,128)(2,1)}, u32[]{:S(2)}) copy-start(bf16[512,512]{1,0:T(8,128)(2,1)} %get-tuple-element.78) | copy-start | bytes 1572868
